TPU v7x, 32 devices: a whole 2x2x4 slice. The times are simulated.
32 devices in a mesh: rep: 4 (over y, x), exp: 8 (over z, core).
Axes of the slice: x: 2, y: 2, z: 4, core: 2. Of those that a mesh axis runs over, the one named last changes fastest.
Arguments:
- features: bfloat16 [4096, 2048], P(('rep', 'exp')), may hold values from -6 to 6
- out_grad: bfloat16 [4096, 2048], P(('rep', 'exp')), may hold values from -1.5 to 1.5
- expert_ids: int32 [4096, 2], P(('rep', 'exp')), may hold values from 0 to 7, all different within a row; in each aligned block of 128 rows (0 to 127, 128 to 255, ...) at most 64 rows name the same one
- gate_probs: bfloat16 [4096, 2], P(('rep', 'exp')), may hold values from 0.049804688 to 0.59765625
- w_gate: bfloat16 [8, 2048, 768], P('exp'), may hold values from -0.125 to 0.125
- w_up: bfloat16 [8, 2048, 768], P('exp'), may hold values from -0.125 to 0.125
- w_down: bfloat16 [8, 2048, 768], P('exp'), may hold values from -0.21875 to 0.21875
Outputs:
- in_grad: bfloat16 [4096, 2048], P(('rep', 'exp'))
- gate_grad: bfloat16 [4096, 2], P(('rep', 'exp'))
- delta_gate: bfloat16 [8, 2048, 768], P('exp', 'rep')
- delta_up: bfloat16 [8, 2048, 768], P('exp', 'rep')
- delta_down: bfloat16 [8, 2048, 768], P('exp', 'rep')
Inputs may be any that keep to these rules, and one draw needn't show every extreme that they name: `expert_ids`: the 2 entries of a token name different experts. Among the 128 tokens of one device (aligned blocks in token order) no expert is named by more than 64 entries, and in every draw some expert is named by exactly 64 entries of some device. Every expert is named somewhere.
All inputs are finite; a program needn't handle non-finite values.
Results may differ from a plain program's by a relative error of at most 0.012.
Values may be sent and summed in bfloat16 or wider, within the bound.
No kernel may reach another device: no remote copies, remote signals or barrier semaphores. Data moves between devices by JAX's collectives and lax.ppermute only.
A program may use at most 128 MiB of HBM per device.

v0:
```python
import jax
import jax.numpy as jnp
from jax import lax
from jax.sharding import PartitionSpec as P


def dot_rows(matrix_a, matrix_b):
    return lax.dot_general(
        matrix_a, matrix_b, (((0,), (0,)), ((), ())), preferred_element_type=jnp.float32
    )


def dot_last(matrix_a, matrix_b):
    return lax.dot_general(
        matrix_a, matrix_b, (((1,), (1,)), ((), ())), preferred_element_type=jnp.float32
    )


def expert_terms(inputs, gate_mat, up_mat, down_mat):
    rows_x, rows_dy, rows_g = inputs
    pre_gate = jnp.dot(rows_x, gate_mat, preferred_element_type=jnp.float32)
    pre_up = jnp.dot(rows_x, up_mat, preferred_element_type=jnp.float32)
    gate_sig = jax.nn.sigmoid(pre_gate)
    gate_act = pre_gate * gate_sig
    hidden = (gate_act * pre_up).astype(jnp.bfloat16)
    back_grad = jnp.dot(rows_dy, down_mat, preferred_element_type=jnp.float32)
    gate_row = jnp.sum(back_grad * hidden.astype(jnp.float32), axis=1).astype(jnp.bfloat16)
    scaled = (rows_g * rows_dy.astype(jnp.float32)).astype(jnp.bfloat16)
    d_hidden = rows_g * back_grad
    d_gate = (d_hidden * pre_up * gate_sig * (1.0 + pre_gate * (1.0 - gate_sig))).astype(
        jnp.bfloat16
    )
    d_up = (d_hidden * gate_act).astype(jnp.bfloat16)
    row_grad = (dot_last(d_gate, gate_mat) + dot_last(d_up, up_mat)).astype(jnp.bfloat16)
    return (row_grad, gate_row, hidden, scaled, d_gate, d_up)


def on_device(features, out_grad, expert_ids, gate_probs, w_gate, w_up, w_down):
    tokens, model_width = features.shape
    top_k = expert_ids.shape[1]
    hidden_units = w_gate.shape[2]
    experts = lax.axis_size("exp")
    replicas = lax.axis_size("rep")
    capacity = min(tokens, 2 * tokens * top_k // experts)
    flat_ids = expert_ids.reshape(-1)
    one_hot = (flat_ids[:, None] == jnp.arange(experts, dtype=jnp.int32)[None, :]).astype(jnp.int32)
    slot_index = jnp.sum((jnp.cumsum(one_hot, axis=0) - 1) * one_hot, axis=1)
    slot_count_all = experts * capacity
    target = flat_ids * capacity + slot_index
    entries = jnp.arange(tokens * top_k, dtype=jnp.int32)
    picked = jnp.zeros((slot_count_all,), jnp.int32).at[target].set(entries)
    filled = (
        jnp.zeros((slot_count_all,), jnp.bfloat16)
        .at[target]
        .set(jnp.ones((tokens * top_k,), jnp.bfloat16))
    )
    token_idx = picked // top_k
    keep = filled[:, None]
    send_x = (features[token_idx] * keep).reshape(experts, capacity, model_width)
    send_dy = (out_grad[token_idx] * keep).reshape(experts, capacity, model_width)
    send_g = (gate_probs.reshape(-1)[picked] * filled).reshape(experts, capacity)
    gate_mat, up_mat, down_mat = (w_gate[0], w_up[0], w_down[0])
    recv_x = lax.all_to_all(send_x, "exp", split_axis=0, concat_axis=0, tiled=True)
    recv_dy = lax.all_to_all(send_dy, "exp", split_axis=0, concat_axis=0, tiled=True)
    recv_g = lax.all_to_all(send_g, "exp", split_axis=0, concat_axis=0, tiled=True)
    senders, slot_count = recv_g.shape
    row_count = senders * slot_count
    inputs = (
        recv_x.reshape(row_count, model_width),
        recv_dy.reshape(row_count, model_width),
        recv_g.reshape(row_count, 1).astype(jnp.float32),
    )
    row_grad, gate_row, hidden, scaled, d_gate, d_up = expert_terms(
        inputs, gate_mat, up_mat, down_mat
    )
    outputs = (
        row_grad.reshape(senders, slot_count, model_width),
        gate_row.reshape(senders, slot_count),
        hidden.reshape(senders, slot_count, hidden_units),
        scaled.reshape(senders, slot_count, model_width),
        d_gate.reshape(senders, slot_count, hidden_units),
        d_up.reshape(senders, slot_count, hidden_units),
        recv_x,
    )
    returned = (
        lax.all_to_all(outputs[0], "exp", split_axis=0, concat_axis=0, tiled=True),
        lax.all_to_all(outputs[1], "exp", split_axis=0, concat_axis=0, tiled=True),
    )
    results = (returned[0], returned[1]) + outputs[2:]
    h_all = results[2].reshape(-1, hidden_units)
    a_all = results[3].reshape(-1, model_width)
    dg_all = results[4].reshape(-1, hidden_units)
    du_all = results[5].reshape(-1, hidden_units)
    x_all = results[6].reshape(-1, model_width)
    summed = lax.psum_scatter(
        jnp.concatenate(
            [dot_rows(x_all, dg_all), dot_rows(x_all, du_all), dot_rows(a_all, h_all)], axis=1
        ).astype(jnp.bfloat16),
        "rep",
        scatter_dimension=0,
        tiled=True,
    ).astype(jnp.float32)
    returned = (results[0], results[1])
    row_grads = (
        returned[0][flat_ids, slot_index].astype(jnp.float32).reshape(tokens, top_k, model_width)
    )
    in_grad = jnp.sum(row_grads, axis=1).astype(jnp.bfloat16)
    gate_grad = returned[1][flat_ids, slot_index].reshape(tokens, top_k)
    delta_gate = (summed[:, :hidden_units] / replicas).astype(jnp.bfloat16)[None]
    delta_up = (summed[:, hidden_units : 2 * hidden_units] / replicas).astype(jnp.bfloat16)[None]
    delta_down = (summed[:, 2 * hidden_units :] / replicas).astype(jnp.bfloat16)[None]
    return (in_grad, gate_grad, delta_gate, delta_up, delta_down)


def solution(mesh):
    in_specs = (
        P(("rep", "exp"), None),
        P(("rep", "exp"), None),
        P(("rep", "exp"), None),
        P(("rep", "exp"), None),
        P("exp", None, None),
        P("exp", None, None),
        P("exp", None, None),
    )
    out_specs = (
        P(("rep", "exp"), None),
        P(("rep", "exp"), None),
        P("exp", "rep", None),
        P("exp", "rep", None),
        P("exp", "rep", None),
    )
    return jax.shard_map(
        on_device, mesh=mesh, in_specs=in_specs, out_specs=out_specs, check_vma=False
    )
```

profile of v0, /device:TPU:0, one launch (start us, length us, event | category | flops | bytes accessed | tf_op | source)
XLA Modules:
  0.0 279.7 jit_solution(16414680524007555002)
XLA Ops:
  7.2 0.0 copy-start
  7.2 0.9 copy.24
  8.1 0.1 reshape.162
  8.3 0.1 eq.29
  8.4 0.1 eq.25
  8.6 0.6 reduce-window.6
  9.1 0.2 slice_reduce_fusion
  9.4 0.1 fusion.20
  9.5 1.4 scatter_custom_fusion
  10.9 0.8 copy.23
  11.7 0.1 reshape.161
  11.9 2.2 scatter_custom_fusion.1
  14.1 3.4 %gather_fusion = bf16[512]{0:T(512)(128)(2,1)S(1)} fusion(bf16[256]{0:T(256)(128)(2,1)S(1)} %reshape.161, s32[1024]{0:T(1024)S(1)} %get-tuple-element.34), kind=kCustom, calls=%fused_computation | custom fusion | bytes 4096 | tf_op jit(solution)/shard_map/gather | solution.py:61
  17.5 0.7 all_to_all.28
  18.1 6.3 %all-to-all-start = ((bf16[8,1,64]{2,1,0:T(2,128)(2,1)}), bf16[8,1,64]{2,1,0:T(2,128)(2,1)S(1)}, u32[]{:S(2)}, u32[]{:S(2)}) async-start(bf16[8,1,64]{2,1,0:T(2,128)(2,1)} %all_to_all.28), calls=%async_computation | async-start | bytes 8192 | tf_op jit(solution)/shard_map/all_to_all | solution.py:65
  24.5 0.1 mul.78
  24.5 6.4 %gather_fusion.1 = bf16[512,2048]{1,0:T(8,128)(2,1)} fusion(bf16[128,2048]{1,0:T(8,128)(2,1)} %param.8, s32[1024]{0:T(1024)S(1)} %get-tuple-element.33), kind=kCustom, calls=%fused_computation.1 | custom fusion | bytes 4196352 | tf_op jit(solution)/shard_map/gather | solution.py:60
  30.9 6.3 %gather_fusion.2 = bf16[512,2048]{1,0:T(8,128)(2,1)} fusion(bf16[128,2048]{1,0:T(8,128)(2,1)} %param.7, s32[1024]{0:T(1024)S(1)} %get-tuple-element.33), kind=kCustom, calls=%fused_computation.2 | custom fusion | bytes 4196352 | tf_op jit(solution)/shard_map/gather | solution.py:59
  37.3 4.6 %broadcast_multiply_fusion.1 = (bf16[8,64,2048]{2,1,0:T(8,128)(2,1)}, bf16[8,64,2048]{2,1,0:T(8,128)(2,1)}) fusion(bf16[8,64,2048]{2,1,0:T(8,128)(2,1)} %bitcast.53, bf16[8,64]{1,0:T(8,128)(2,1)S(1)} %mul.78, bf16[8,64,2048]{2,1,0:T(8,128)(2,1)} %bitcast.54), kind=kLoop, calls=%fused_computation.37 | loop fusion | flops 2097152 | bytes 8389632 | tf_op jit(solution)/shard_map/mul | solution.py:60
  41.9 0.0 all-to-all-done
  41.9 54.3 %all_to_all.34 = bf16[8,64,2048]{2,1,0:T(8,128)(2,1)} all-to-all(bf16[8,64,2048]{2,1,0:T(8,128)(2,1)} %get-tuple-element.32), channel_id=1, replica_groups=mesh['rep'=4,'exp'=8] {'exp'}, dimensions={0} | all-to-all | bytes 4194304 | tf_op jit(solution)/shard_map/all_to_all | solution.py:63
  96.2 4.3 %all-to-all-start.1 = ((bf16[8,64,2048]{2,1,0:T(8,128)(2,1)}), bf16[8,64,2048]{2,1,0:T(8,128)(2,1)}, u32[]{:S(2)}, u32[]{:S(2)}) async-start(bf16[8,64,2048]{2,1,0:T(8,128)(2,1)} %get-tuple-element.31), calls=%async_computation.1 | async-start | bytes 4194304 | tf_op jit(solution)/shard_map/all_to_all | solution.py:64
  100.5 0.2 reduce-scatter.2.cloned.1.call-start
  100.7 0.1 reshape.168
  100.8 5.6 %fusion.6 = f32[512,768]{1,0:T(8,128)} fusion(bf16[512,2048]{1,0:T(8,128)(2,1)} %bitcast.55, bf16[1,2048,768]{2,1,0:T(8,128)(2,1)} %param.12), kind=kOutput, calls=%fused_computation.19 | convolution fusion | flops 1610612736 | bytes 6815744 | tf_op jit(solution)/shard_map/dot_general | solution.py:22
  106.4 0.0 copy-done
  106.4 0.0 copy-done.1
  106.4 3.0 %fusion.2 = f32[512,768]{1,0:T(8,128)} fusion(bf16[512,2048]{1,0:T(8,128)(2,1)S(1)} %bitcast.56, bf16[1,2048,768]{2,1,0:T(8,128)(2,1)S(1)} %copy-done), kind=kOutput, calls=%fused_computation.15 | convolution fusion | flops 1610612736 | bytes 6815744 | tf_op jit(solution)/shard_map/dot_general | solution.py:21
  109.4 40.1 %all-to-all-done.1 = bf16[8,64,2048]{2,1,0:T(8,128)(2,1)} async-done(((bf16[8,64,2048]{2,1,0:T(8,128)(2,1)}), bf16[8,64,2048]{2,1,0:T(8,128)(2,1)}, u32[]{:S(2)}, u32[]{:S(2)}) %all-to-all-start.1) | async-done | bytes 2097184 | tf_op jit(solution)/shard_map/all_to_all | solution.py:64
  149.6 5.8 %multiply_reduce_fusion = (bf16[512]{0:T(512)(128)(2,1)S(1)}, bf16[512,768]{1,0:T(8,128)(2,1)S(1)}, bf16[512,768]{1,0:T(8,128)(2,1)S(1)}, bf16[512,768]{1,0:T(8,128)(2,1)S(1)}) fusion(f32[512,768]{1,0:T(8,128)} %fusion.6, f32[512,768]{1,0:T(8,128)} %fusion.2, f32[512]{0:T(512)S(1)} %reshape.168, bf16[512,2048]{1,0:T(8,128)(2,1)} %bitcast.5, ...), kind=kOutput, calls=%fused_computation.30 | convolution fusion | flops 1618083328 | bytes 10750976 | tf_op jit(solution)/shard_map/dot_general | solution.py:26
  155.4 0.0 copy-start.4
  155.4 0.0 copy-start.6
  155.4 0.0 copy-start.2
  155.4 4.1 %convolution_convert_fusion = bf16[2048,768]{0,1:T(8,128)(2,1)S(1)} fusion(bf16[512,768]{1,0:T(8,128)(2,1)S(1)} %get-tuple-element.21, bf16[512,2048]{1,0:T(8,128)(2,1)} %bitcast.5, f32[512]{0:T(512)S(1)} %reshape.168), kind=kOutput, calls=%fused_computation.10 | convolution fusion | flops 1615331328 | bytes 6031360 | tf_op jit(solution)/shard_map/dot_general | solution.py:8
  159.5 0.0 copy-done.4
  159.5 0.0 copy-done.2
  159.6 1.9 convolution_convert_fusion.1
  161.4 0.0 copy-done.6
  161.4 1.9 convolution_convert_fusion.2
  163.3 4.5 %pad_maximum_fusion = bf16[2048,2304]{0,1:T(8,128)(2,1)} fusion(bf16[2048,768]{0,1:T(8,128)(2,1)S(1)} %convolution_convert_fusion, bf16[2048,768]{0,1:T(8,128)(2,1)S(1)} %convolution_convert_fusion.1, bf16[2048,768]{0,1:T(8,128)(2,1)S(1)} %convolution_convert_fusion.2), kind=kLoop, calls=%fused_computation.7 | loop fusion | flops 28311552 | bytes 18874368 | tf_op jit(solution)/shard_map/concatenate | solution.py:96
  167.8 0.0 reduce-scatter.2.cloned.1.call-update
  167.8 0.7 convert_element_type.84
  168.5 3.5 %all-to-all-start.4 = ((bf16[8,1,64]{2,1,0:T(2,128)(2,1)}), bf16[8,1,64]{2,1,0:T(2,128)(2,1)S(1)}, u32[]{:S(2)}, u32[]{:S(2)}) async-start(bf16[8,1,64]{2,1,0:T(2,128)(2,1)} %convert_element_type.84), calls=%async_computation.4 | async-start | bytes 8192 | tf_op jit(solution)/shard_map/all_to_all | solution.py:87
  172.0 0.0 copy-start.3
  172.0 0.0 copy-start.5
  172.1 3.2 %fusion = f32[512,2048]{1,0:T(8,128)S(1)} fusion(bf16[512,768]{1,0:T(8,128)(2,1)} %copy-done.6, bf16[1,2048,768]{2,1,0:T(8,128)(2,1)S(1)} %copy-done), kind=kOutput, calls=%fused_computation.13 | convolution fusion | flops 1610612736 | bytes 8126464 | tf_op jit(solution)/shard_map/dot_general | solution.py:14
  175.2 0.0 copy-done.3
  175.2 0.0 copy-done.5
  175.2 3.1 %add_convert_fusion = bf16[512,2048]{1,0:T(8,128)(2,1)} fusion(f32[512,2048]{1,0:T(8,128)S(1)} %fusion, bf16[512,768]{1,0:T(8,128)(2,1)S(1)} %copy-done.5, bf16[1,2048,768]{2,1,0:T(8,128)(2,1)S(1)} %copy-done.3), kind=kOutput, calls=%fused_computation.9 | convolution fusion | flops 1612709888 | bytes 10223616 | tf_op jit(solution)/shard_map/dot_general | solution.py:14
  178.4 0.0 all-to-all-done.4
  178.4 4.7 %all-to-all-start.3 = ((bf16[8,64,2048]{2,1,0:T(8,128)(2,1)}), bf16[8,64,2048]{2,1,0:T(8,128)(2,1)}, u32[]{:S(2)}, u32[]{:S(2)}) async-start(bf16[8,64,2048]{2,1,0:T(8,128)(2,1)} %bitcast.59), calls=%async_computation.3 | async-start | bytes 4194304 | tf_op jit(solution)/shard_map/all_to_all | solution.py:86
  183.1 2.4 gather_fusion.4
  185.5 0.2 reshape.167
  185.7 0.6 copy.29
  186.3 46.0 %all-to-all-done.3 = bf16[8,64,2048]{2,1,0:T(8,128)(2,1)} async-done(((bf16[8,64,2048]{2,1,0:T(8,128)(2,1)}), bf16[8,64,2048]{2,1,0:T(8,128)(2,1)}, u32[]{:S(2)}, u32[]{:S(2)}) %all-to-all-start.3) | async-done | bytes 2097184 | tf_op jit(solution)/shard_map/all_to_all | solution.py:86
  232.3 5.2 %gather_fusion.3 = bf16[256,2048]{1,0:T(8,128)(2,1)} fusion(bf16[8,64,2048]{2,1,0:T(8,128)(2,1)} %all-to-all-done.3, s32[256]{0:T(256)S(1)} %bitcast.52), kind=kCustom, calls=%fused_computation.3 | custom fusion | bytes 2099200 | tf_op jit(solution)/shard_map/gather | solution.py:105
  237.5 2.5 gather.27
  240.0 4.6 %reduce_sum.34 = bf16[128,2048]{1,0:T(8,128)(2,1)} reduce(bf16[128,2,2048]{2,1,0:T(2,128)(2,1)} %gather.27, bf16[]{:T(256)} %constant.39.clone.1), dimensions={1}, to_apply=%region_5.6 | reduce | flops 262144 | bytes 1572866 | tf_op jit(solution)/shard_map/reduce_sum | solution.py:107
  244.6 17.3 %reduce-scatter.2.cloned.1.call-done = bf16[512,2304]{0,1:T(8,128)(2,1)} async-done(((bf16[2048,2304]{0,1:T(8,128)(2,1)}), bf16[512,2304]{0,1:T(8,128)(2,1)}) %reduce-scatter.2.cloned.1.call-update) | async-done | bytes 2359312 | tf_op jit(solution)/shard_map/reduce_scatter | solution.py:95
  261.8 2.3 convert_element_type.79
  264.2 1.8 fusion.19
  266.0 2.3 copy.30
  268.2 2.3 copy.31
  270.5 2.3 copy.32
  (12 shorter events, 0.1 us)
Async XLA Ops:
  7.2 99.3 %copy-start = (bf16[1,2048,768]{2,1,0:T(8,128)(2,1)S(1)}, bf16[1,2048,768]{2,1,0:T(8,128)(2,1)}, u32[]{:S(2)}) copy-start(bf16[1,2048,768]{2,1,0:T(8,128)(2,1)} %param.11) | copy-start | bytes 9437188
  18.1 23.8 %all-to-all-start = ((bf16[8,1,64]{2,1,0:T(2,128)(2,1)}), bf16[8,1,64]{2,1,0:T(2,128)(2,1)S(1)}, u32[]{:S(2)}, u32[]{:S(2)}) async-start(bf16[8,1,64]{2,1,0:T(2,128)(2,1)} %all_to_all.28), calls=%async_computation | async-start | bytes 8192 | tf_op jit(solution)/shard_map/all_to_all | solution.py:65
  96.2 53.4 %all-to-all-start.1 = ((bf16[8,64,2048]{2,1,0:T(8,128)(2,1)}), bf16[8,64,2048]{2,1,0:T(8,128)(2,1)}, u32[]{:S(2)}, u32[]{:S(2)}) async-start(bf16[8,64,2048]{2,1,0:T(8,128)(2,1)} %get-tuple-element.31), calls=%async_computation.1 | async-start | bytes 4194304 | tf_op jit(solution)/shard_map/all_to_all | solution.py:64
  100.5 161.3 %reduce-scatter.2.cloned.1.call-start = ((), (), s32[]{:S(2)}) async-start(), calls=%async_computation.6 | async-start | bytes 11796480 | tf_op jit(solution)/shard_map/reduce_scatter | solution.py:95
  100.8 5.6 %copy-start.1 = (bf16[8,64,2048]{2,1,0:T(8,128)(2,1)S(1)}, bf16[8,64,2048]{2,1,0:T(8,128)(2,1)}, u32[]{:S(2)}) copy-start(bf16[8,64,2048]{2,1,0:T(8,128)(2,1)} %all_to_all.34) | copy-start | bytes 6291460
  155.4 4.2 %copy-start.4 = (bf16[512,768]{1,0:T(8,128)(2,1)}, bf16[512,768]{1,0:T(8,128)(2,1)S(1)}, u32[]{:S(2)}) copy-start(bf16[512,768]{1,0:T(8,128)(2,1)S(1)} %get-tuple-element.26) | copy-start | bytes 2359300
  155.4 6.0 %copy-start.6 = (bf16[512,768]{1,0:T(8,128)(2,1)}, bf16[512,768]{1,0:T(8,128)(2,1)S(1)}, u32[]{:S(2)}) copy-start(bf16[512,768]{1,0:T(8,128)(2,1)S(1)} %get-tuple-element.25) | copy-start | bytes 2359300
  155.4 4.2 %copy-start.2 = (bf16[8,64,2048]{2,1,0:T(8,128)(2,1)S(1)}, bf16[8,64,2048]{2,1,0:T(8,128)(2,1)}, u32[]{:S(2)}) copy-start(bf16[8,64,2048]{2,1,0:T(8,128)(2,1)} %all_to_all.34) | copy-start | bytes 6291460
  168.5 9.9 %all-to-all-start.4 = ((bf16[8,1,64]{2,1,0:T(2,128)(2,1)}), bf16[8,1,64]{2,1,0:T(2,128)(2,1)S(1)}, u32[]{:S(2)}, u32[]{:S(2)}) async-start(bf16[8,1,64]{2,1,0:T(2,128)(2,1)} %convert_element_type.84), calls=%async_computation.4 | async-start | bytes 8192 | tf_op jit(solution)/shard_map/all_to_all | solution.py:87
  172.0 3.2 %copy-start.3 = (bf16[1,2048,768]{2,1,0:T(8,128)(2,1)S(1)}, bf16[1,2048,768]{2,1,0:T(8,128)(2,1)}, u32[]{:S(2)}) copy-start(bf16[1,2048,768]{2,1,0:T(8,128)(2,1)} %param.12) | copy-start | bytes 9437188
  172.0 3.2 %copy-start.5 = (bf16[512,768]{1,0:T(8,128)(2,1)S(1)}, bf16[512,768]{1,0:T(8,128)(2,1)}, u32[]{:S(2)}) copy-start(bf16[512,768]{1,0:T(8,128)(2,1)} %copy-done.4) | copy-start | bytes 2359300
  178.4 53.9 %all-to-all-start.3 = ((bf16[8,64,2048]{2,1,0:T(8,128)(2,1)}), bf16[8,64,2048]{2,1,0:T(8,128)(2,1)}, u32[]{:S(2)}, u32[]{:S(2)}) async-start(bf16[8,64,2048]{2,1,0:T(8,128)(2,1)} %bitcast.59), calls=%async_computation.3 | async-start | bytes 4194304 | tf_op jit(solution)/shard_map/all_to_all | solution.py:86
Sparse Core Ops, SparseCore 0:
  167.9 93.8 reduce-scatter.1
where the time goes:
time: 280 us
  waiting for transfers between devices  103 us (37%)
  blocking collectives  54.3 us (19%)
  local copies, waits for them, and re-layouts  41.4 us (15%)
  matrix products  28.6 us (10%)
  starting transfers between devices  19.1 us (7%)
  other arithmetic  18.5 us (7%)
  between operations  14.3 us (5%)
    all_to_all x1, blocking collectives, on_device(): lax.all_to_all(send_x, 'exp', split_axis=0, concat_axis=0, tiled=True)  54.3 us
    all_to_all x1, waiting for transfers between devices, on_device(): lax.all_to_all(outputs[0], 'exp', split_axis=0, concat_axis=0, tiled=True)  46 us
    all_to_all x1, waiting for transfers between devices, on_device(): lax.all_to_all(send_dy, 'exp', split_axis=0, concat_axis=0, tiled=True)  40.1 us
    reduce_scatter x1, waiting for transfers between devices, on_device(): lax.psum_scatter(jnp.concatenate([dot_rows(x_all, dg_all), dot_rows(x_all...  17.3 us
    unnamed x21, local copies, waits for them, and re-layouts  9.23 us
    dot_general x3, matrix products, dot_rows(): lax.dot_general(matrix_a, matrix_b, (((0,), (0,)), ((), ())), preferred_e...  7.86 us
    gather x2, local copies, waits for them, and re-layouts, on_device(): returned[0][flat_ids, slot_index].astype(jnp.float32)  7.7 us
    gather x1, local copies, waits for them, and re-layouts, on_device(): out_grad[token_idx] * keep  6.4 us
  transfers between devices with their start and end apart: 5, of which 3 were waited for; matrix products, arithmetic and copies ran while one was open for 17% of the time, Pallas kernels for 0%

commit v1 on v0

v1 whole, which is shorter than its diff:
```python
import jax
import jax.numpy as jnp
from jax import lax
from jax.sharding import PartitionSpec as P

F32 = jnp.float32
BF16 = jnp.bfloat16


def dot_rows(matrix_a, matrix_b):
    return lax.dot_general(
        matrix_a, matrix_b, (((0,), (0,)), ((), ())), preferred_element_type=F32
    )


def dot_last(matrix_a, matrix_b):
    return lax.dot_general(
        matrix_a, matrix_b, (((1,), (1,)), ((), ())), preferred_element_type=F32
    )


def route(meta, tokens, top_k, capacity):
    senders = meta.shape[0] // tokens
    me = lax.axis_index("exp")
    ids = meta[:, :top_k].reshape(senders, tokens, top_k)
    probs = meta[:, top_k:].reshape(senders, tokens, top_k)
    hit = ids == me.astype(BF16)
    named = jnp.any(hit, axis=2)
    gate = jnp.sum(jnp.where(hit, probs, 0).astype(F32), axis=2)
    upto = (jnp.arange(tokens)[:, None] <= jnp.arange(tokens)[None, :]).astype(BF16)
    rank = jnp.dot(named.astype(BF16), upto, preferred_element_type=F32) - 1.0
    slots = jnp.arange(capacity, dtype=F32)
    chosen = named[:, None, :] & (rank[:, None, :] == slots[None, :, None])
    rows_g = jnp.sum(jnp.where(chosen, gate[:, None, :], 0.0), axis=2)
    return hit, chosen, rows_g.reshape(senders * capacity, 1)


def pick(select, dense):
    senders, capacity, tokens = select.shape
    rows = lax.dot_general(
        select,
        dense.reshape(senders, tokens, -1),
        (((2,), (1,)), ((0,), (0,))),
        preferred_element_type=F32,
    )
    return rows.astype(BF16).reshape(senders * capacity, -1)


def spread(select, rows):
    senders, capacity, tokens = select.shape
    dense = lax.dot_general(
        select,
        rows.reshape(senders, capacity, -1),
        (((1,), (1,)), ((0,), (0,))),
        preferred_element_type=F32,
    )
    return dense.astype(BF16).reshape(senders * tokens, -1)


def on_device(features, out_grad, expert_ids, gate_probs, w_gate, w_up, w_down):
    tokens, model_width = features.shape
    top_k = expert_ids.shape[1]
    experts = lax.axis_size("exp")
    replicas = lax.axis_size("rep")
    capacity = min(tokens, 2 * tokens * top_k // experts)
    gate_mat, up_mat, down_mat = (w_gate[0], w_up[0], w_down[0])

    meta = jnp.concatenate([expert_ids.astype(BF16), gate_probs], axis=1)
    meta = lax.all_gather(meta, "exp", axis=0, tiled=True)
    all_x = lax.all_gather(features, "exp", axis=0, tiled=True)
    all_dy = lax.all_gather(out_grad, "exp", axis=0, tiled=True)

    hit, chosen, rows_g = route(meta, tokens, top_k, capacity)
    select = chosen.astype(BF16)
    rows_x = pick(select, all_x)
    pre_gate = jnp.dot(rows_x, gate_mat, preferred_element_type=F32)
    pre_up = jnp.dot(rows_x, up_mat, preferred_element_type=F32)
    gate_sig = jax.nn.sigmoid(pre_gate)
    gate_act = pre_gate * gate_sig
    hidden = (gate_act * pre_up).astype(BF16)

    rows_dy = pick(select, all_dy)
    back_grad = jnp.dot(rows_dy, down_mat, preferred_element_type=F32)
    gate_row = jnp.sum(back_grad * hidden.astype(F32), axis=1).astype(BF16)
    scaled = (rows_g * rows_dy.astype(F32)).astype(BF16)
    d_hidden = rows_g * back_grad
    d_gate = (d_hidden * pre_up * gate_sig * (1.0 + pre_gate * (1.0 - gate_sig))).astype(BF16)
    d_up = (d_hidden * gate_act).astype(BF16)

    def delta(left, right):
        part = dot_rows(left, right).astype(BF16)
        total = lax.psum_scatter(part, "rep", scatter_dimension=0, tiled=True)
        return (total.astype(F32) / replicas).astype(BF16)[None]

    delta_down = delta(scaled, hidden)
    delta_gate = delta(rows_x, d_gate)
    delta_up = delta(rows_x, d_up)

    row_grad = (dot_last(d_gate, gate_mat) + dot_last(d_up, up_mat)).astype(BF16)
    in_grad = lax.psum_scatter(
        spread(select, row_grad), "exp", scatter_dimension=0, tiled=True
    )
    gate_dense = jnp.sum(
        jnp.where(chosen, gate_row.astype(F32).reshape(experts, capacity, 1), 0.0), axis=1
    )
    gate_dense = jnp.where(hit, gate_dense[:, :, None], 0.0).astype(BF16)
    gate_grad = lax.psum_scatter(
        gate_dense.reshape(experts * tokens, top_k), "exp", scatter_dimension=0, tiled=True
    )
    return (in_grad, gate_grad, delta_gate, delta_up, delta_down)


def solution(mesh):
    by_token = P(("rep", "exp"), None)
    by_expert = P("exp", None, None)
    by_shard = P("exp", "rep", None)
    return jax.shard_map(
        on_device,
        mesh=mesh,
        in_specs=(by_token,) * 4 + (by_expert,) * 3,
        out_specs=(by_token,) * 2 + (by_shard,) * 3,
        check_vma=False,
    )
```

time: 280 us -> 349 us (1.25)
  waiting for transfers between devices: 103 us -> 266 us
  blocking collectives: 54.3 us -> 13.4 us
  local copies, waits for them, and re-layouts: 41.4 us -> 4.73 us
  starting transfers between devices: 19.1 us -> 0.46 us
  matrix products: 28.6 us -> 36.8 us
  other arithmetic: 18.5 us -> 12.2 us
    reduce_scatter x1 -> x4, waiting for transfers between devices: 17.3 us -> 185 us  [the longest x3 134 us: delta(): total = lax.psum_scatter(part, 'rep', scatter_dimension=0, tiled=True)]
    all_to_all x4 -> x0, waiting for transfers between devices: 86.1 us -> none  [the longest x1 46 us: on_device(): lax.all_to_all(outputs[0], 'exp', split_axis=0, concat_axis=0, tiled=True)]
    all_gather x0 -> x2, waiting for transfers between devices: none -> 79.1 us  [the longest x1 43.3 us: on_device(): all_dy = lax.all_gather(out_grad, 'exp', axis=0, tiled=True)]
    all_to_all x1 -> x0, blocking collectives: 54.3 us -> none  [on_device(): lax.all_to_all(send_x, 'exp', split_axis=0, concat_axis=0, tiled=True)]
    gather x6 -> x0, local copies, waits for them, and re-layouts: 26.2 us -> none  [the longest x2 7.7 us: on_device(): returned[0][flat_ids, slot_index].astype(jnp.float32)]
    all_to_all x4 -> x0, starting transfers between devices: 18.9 us -> none  [the longest x1 6.33 us: on_device(): lax.all_to_all(send_g, 'exp', split_axis=0, concat_axis=0, tiled=True)]
    all_gather x0 -> x1, blocking collectives: none -> 13.4 us  [on_device(): meta = lax.all_gather(meta, 'exp', axis=0, tiled=True)]
    dot_general x3, matrix products: 7.86 us -> 14.3 us  [dot_rows(): lax.dot_general(matrix_a, matrix_b, (((0,), (0,)), ((), ())), preferred_e...]
  transfers between devices with their start and end apart: 5 -> 7, of which waited for: 3 -> 7; matrix products, arithmetic and copies ran while one was open for 17% -> 12% of each run, Pallas kernels for 0% -> 0%
where the time goes in v1:
time: 349 us; the launch traced here: 348 us
  waiting for transfers between devices  266 us (76%)
  matrix products  36.8 us (11%)
  between operations  14.3 us (4%)
  blocking collectives  13.4 us (4%)
  other arithmetic  12.2 us (3%)
  local copies, waits for them, and re-layouts  4.73 us (1%)
    reduce_scatter x3, waiting for transfers between devices, delta(): total = lax.psum_scatter(part, 'rep', scatter_dimension=0, tiled=True)  134 us
    reduce_scatter x1, waiting for transfers between devices, on_device(): lax.psum_scatter(spread(select, row_grad), 'exp', scatter_dimension=0, ti...  50.9 us
    all_gather x1, waiting for transfers between devices, on_device(): all_dy = lax.all_gather(out_grad, 'exp', axis=0, tiled=True)  43.3 us
    all_gather x1, waiting for transfers between devices, on_device(): all_x = lax.all_gather(features, 'exp', axis=0, tiled=True)  35.8 us
    dot_general x3, matrix products, dot_rows(): lax.dot_general(matrix_a, matrix_b, (((0,), (0,)), ((), ())), preferred_e...  14.3 us
    all_gather x1, blocking collectives, on_device(): meta = lax.all_gather(meta, 'exp', axis=0, tiled=True)  13.4 us
    dot_general x2, matrix products, pick(): lax.dot_general(select, dense.reshape(senders, tokens, -1), (((2,), (1,))...  7.23 us
  transfers between devices with their start and end apart: 7, of which 7 were waited for; matrix products, arithmetic and copies ran while one was open for 12% of the time, Pallas kernels for 0%

profile of v1, /device:TPU:0, one launch (start us, length us, event | category | flops | bytes accessed | tf_op | source)
XLA Modules:
  0.0 348.4 jit_solution(11412678350528004462)
XLA Ops:
  7.2 0.0 copy-start
  7.2 0.0 all-gather.5.cloned.1.call-start
  7.2 0.7 all-gather.5.cloned.1.call-update
  7.9 0.0 all-gather.3.cloned.1.call-start
  8.0 0.7 all-gather.3.cloned.1.call-update
  8.7 0.0 reduce-scatter.16.cloned.1.call-start
  8.7 0.7 convert_element_type.94
  9.4 0.7 pad_maximum_fusion
  10.1 13.4 %all_gather.9 = bf16[1024,4]{0,1:T(4,128)(2,1)S(1)} all-gather(bf16[128,4]{0,1:T(4,128)(2,1)S(1)} %pad_maximum_fusion), channel_id=1, replica_groups=mesh['rep'=4,'exp'=8] {'exp'}, dimensions={0}, use_global_device_ids=true | all-gather | bytes 9216 | tf_op jit(solution)/shard_map/all_gather | solution.py:69
  23.5 0.1 convolution_add_fusion
  23.7 35.8 %all-gather.5.cloned.1.call-done = bf16[1024,2048]{1,0:T(8,128)(2,1)} async-done(((bf16[128,2048]{1,0:T(8,128)(2,1)}), bf16[1024,2048]{1,0:T(8,128)(2,1)}) %all-gather.5.cloned.1.call-update) | async-done | bytes 4194320 | tf_op jit(solution)/shard_map/all_gather | solution.py:70
  59.5 4.2 %convolution_convert_fusion.4 = bf16[8,64,2048]{2,1,0:T(8,128)(2,1)} fusion(bf16[8,128,2048]{2,1,0:T(8,128)(2,1)} %bitcast.49, f32[8,128]{1,0:T(8,128)S(1)} %convolution_add_fusion, pred[8,128]{1,0:T(8,128)(4,1)S(1)} %bitcast.58), kind=kOutput, calls=%fused_computation.16 | convolution fusion | flops 269615104 | bytes 6296576 | tf_op jit(solution)/shard_map/dot_general | solution.py:40
  63.7 43.3 %all-gather.3.cloned.1.call-done = bf16[1024,2048]{1,0:T(8,128)(2,1)} async-done(((bf16[128,2048]{1,0:T(8,128)(2,1)}), bf16[1024,2048]{1,0:T(8,128)(2,1)}) %all-gather.3.cloned.1.call-update) | async-done | bytes 4194320 | tf_op jit(solution)/shard_map/all_gather | solution.py:71
  107.0 0.0 copy-start.1
  107.0 3.0 convolution_convert_fusion.5
  110.0 0.0 copy-start.3
  110.0 0.0 copy-done
  110.1 0.0 copy-done.1
  110.1 0.0 copy-start.9
  110.1 1.8 fusion.2
  111.9 0.8 copy-done.9
  112.7 1.8 fusion.6
  114.5 0.0 copy-start.5
  114.5 0.0 copy-done.3
  114.5 0.0 copy-done.4
  114.5 0.6 copy-done.8
  115.2 3.4 multiply_reduce_fusion
  118.5 0.0 copy-done.5
  118.5 0.1 reshape.59
  118.6 0.2 select_reduce_fusion
  118.9 0.1 mul.42
  118.9 0.9 copy.12
  119.8 0.0 reduce-scatter.16.cloned.1.call-update
  119.8 0.0 reduce-scatter.14.cloned.1.call-start
  119.9 5.4 %convolution_convert_fusion.1 = bf16[2048,768]{1,0:T(8,128)(2,1)} fusion(bf16[512,768]{1,0:T(8,128)(2,1)} %get-tuple-element.8, bf16[512,2048]{1,0:T(8,128)(2,1)} %bitcast.56, f32[512]{0:T(512)S(1)} %mul.42), kind=kOutput, calls=%fused_computation.3 | convolution fusion | flops 1615331328 | bytes 6031360 | tf_op jit(solution)/shard_map/dot_general | solution.py:11
  125.3 0.0 reduce-scatter.14.cloned.1.call-update
  125.3 0.0 reduce-scatter.12.cloned.1.call-start
  125.3 0.0 copy-start.2
  125.4 4.1 %multiply_convert_fusion.6 = (bf16[512,768]{1,0:T(8,128)(2,1)S(1)}, bf16[512,768]{1,0:T(8,128)(2,1)}) fusion(f32[512,768]{1,0:T(8,128)} %get-tuple-element.11, f32[512]{0:T(512)S(1)} %mul.42, f32[512,768]{1,0:T(8,128)} %copy-done.4, f32[512,768]{1,0:T(8,128)} %copy-done.5), kind=kLoop, calls=%fused_computation.24 | loop fusion | flops 5505024 | bytes 6293504 | tf_op jit(solution)/shard_map/convert_element_type | solution.py:88
  129.5 0.9 copy-done.6
  130.4 0.0 copy-done.2
  130.4 3.6 %convolution_convert_fusion.2 = bf16[2048,768]{1,0:T(8,128)(2,1)} fusion(bf16[512,2048]{1,0:T(8,128)(2,1)S(1)} %bitcast.54, bf16[512,768]{1,0:T(8,128)(2,1)S(1)} %get-tuple-element.9), kind=kOutput, calls=%fused_computation.4 | convolution fusion | flops 1612185600 | bytes 6029312 | tf_op jit(solution)/shard_map/dot_general | solution.py:11
  134.0 0.0 reduce-scatter.12.cloned.1.call-update
  134.0 0.2 reduce-scatter.10.cloned.1.call-start
  134.2 5.3 %convolution_convert_fusion.3 = bf16[2048,768]{1,0:T(8,128)(2,1)} fusion(bf16[512,2048]{1,0:T(8,128)(2,1)} %bitcast.51, bf16[512,768]{1,0:T(8,128)(2,1)} %get-tuple-element.10), kind=kOutput, calls=%fused_computation.5 | convolution fusion | flops 1612185600 | bytes 6029312 | tf_op jit(solution)/shard_map/dot_general | solution.py:11
  139.6 0.0 reduce-scatter.10.cloned.1.call-update
  139.6 0.0 reduce-scatter.8.cloned.1.call-start
  139.6 0.0 copy-start.7
  139.6 0.0 copy-start.10
  139.7 3.1 fusion
  142.8 0.0 copy-done.7
  142.8 0.0 copy-done.10
  142.8 1.8 add_convert_fusion
  144.6 3.2 convolution_convert_fusion
  147.9 0.0 reduce-scatter.8.cloned.1.call-update
  147.9 1.2 reduce-scatter.16.cloned.1.call-done
  149.1 1.3 copy.13
  150.4 43.9 %reduce-scatter.14.cloned.1.call-done = bf16[512,768]{1,0:T(8,128)(2,1)} async-done(((bf16[2048,768]{1,0:T(8,128)(2,1)}), bf16[512,768]{1,0:T(8,128)(2,1)}) %reduce-scatter.14.cloned.1.call-update) | async-done | bytes 786448 | tf_op jit(solution)/shard_map/reduce_scatter | solution.py:92
  194.3 2.1 fusion.16
  196.5 44.9 %reduce-scatter.12.cloned.1.call-done = bf16[512,768]{1,0:T(8,128)(2,1)} async-done(((bf16[2048,768]{1,0:T(8,128)(2,1)}), bf16[512,768]{1,0:T(8,128)(2,1)}) %reduce-scatter.12.cloned.1.call-update) | async-done | bytes 786448 | tf_op jit(solution)/shard_map/reduce_scatter | solution.py:92
  241.4 2.1 fusion.15
  243.6 45.0 %reduce-scatter.10.cloned.1.call-done = bf16[512,768]{1,0:T(8,128)(2,1)} async-done(((bf16[2048,768]{1,0:T(8,128)(2,1)}), bf16[512,768]{1,0:T(8,128)(2,1)}) %reduce-scatter.10.cloned.1.call-update) | async-done | bytes 786448 | tf_op jit(solution)/shard_map/reduce_scatter | solution.py:92
  288.5 2.1 fusion.14
  290.7 50.9 %reduce-scatter.8.cloned.1.call-done = bf16[128,2048]{1,0:T(8,128)(2,1)} async-done(((bf16[1024,2048]{1,0:T(8,128)(2,1)}), bf16[128,2048]{1,0:T(8,128)(2,1)}) %reduce-scatter.8.cloned.1.call-update) | async-done | bytes 524304 | tf_op jit(solution)/shard_map/reduce_scatter | solution.py:100
  (6 shorter events, 0.1 us)
Async XLA Ops:
  7.2 102.9 %copy-start = (bf16[1,2048,768]{2,1,0:T(8,128)(2,1)S(1)}, bf16[1,2048,768]{2,1,0:T(8,128)(2,1)}, u32[]{:S(2)}) copy-start(bf16[1,2048,768]{2,1,0:T(8,128)(2,1)} %param.11) | copy-start | bytes 9437188
  7.2 52.3 %all-gather.5.cloned.1.call-start = ((), (), s32[]{:S(2)}) async-start(), calls=%async_computation.6 | async-start | bytes 4718592 | tf_op jit(solution)/shard_map/all_gather | solution.py:70
  7.9 99.1 %all-gather.3.cloned.1.call-start = ((), (), s32[]{:S(2)}) async-start(), calls=%async_computation.5 | async-start | bytes 4718592 | tf_op jit(solution)/shard_map/all_gather | solution.py:71
  8.7 140.4 %reduce-scatter.16.cloned.1.call-start = ((), (), s32[]{:S(2)}) async-start(), calls=%async_computation.11 | async-start | bytes 294912
  107.0 3.1 copy-start.1
  110.0 4.5 %copy-start.3 = (bf16[8,64,2048]{2,1,0:T(8,128)(2,1)}, bf16[8,64,2048]{2,1,0:T(8,128)(2,1)S(1)}, u32[]{:S(2)}) copy-start(bf16[8,64,2048]{2,1,0:T(8,128)(2,1)S(1)} %convolution_convert_fusion.5) | copy-start | bytes 6291460
  110.1 2.6 copy-start.9
  112.7 1.8 copy-start.4
  112.7 2.5 copy-start.8
  114.5 4.0 %copy-start.5 = (f32[512,768]{1,0:T(8,128)}, f32[512,768]{1,0:T(8,128)S(1)}, u32[]{:S(2)}) copy-start(f32[512,768]{1,0:T(8,128)S(1)} %fusion.6) | copy-start | bytes 4718596
  119.8 74.5 %reduce-scatter.14.cloned.1.call-start = ((), (), s32[]{:S(2)}) async-start(), calls=%async_computation.10 | async-start | bytes 3932160 | tf_op jit(solution)/shard_map/reduce_scatter | solution.py:92
  125.3 116.1 %reduce-scatter.12.cloned.1.call-start = ((), (), s32[]{:S(2)}) async-start(), calls=%async_computation.9 | async-start | bytes 3932160 | tf_op jit(solution)/shard_map/reduce_scatter | solution.py:92
  125.3 5.0 %copy-start.2 = (bf16[8,64,2048]{2,1,0:T(8,128)(2,1)S(1)}, bf16[8,64,2048]{2,1,0:T(8,128)(2,1)}, u32[]{:S(2)}) copy-start(bf16[8,64,2048]{2,1,0:T(8,128)(2,1)} %convolution_convert_fusion.4) | copy-start | bytes 6291460
  129.5 0.9 copy-start.6
  134.0 154.5 %reduce-scatter.10.cloned.1.call-start = ((), (), s32[]{:S(2)}) async-start(), calls=%async_computation.8 | async-start | bytes 3932160 | tf_op jit(solution)/shard_map/reduce_scatter | solution.py:92
  139.6 201.9 %reduce-scatter.8.cloned.1.call-start = ((), (), s32[]{:S(2)}) async-start(), calls=%async_computation.7 | async-start | bytes 4718592 | tf_op jit(solution)/shard_map/reduce_scatter | solution.py:100
  139.6 3.1 copy-start.7
  139.6 3.1 copy-start.10
Sparse Core Ops, SparseCore 0:
  9.6 49.8 all-gather.4
  61.1 45.8 all-gather.2
  120.0 29.0 reduce-scatter.15
  152.2 42.0 reduce-scatter.13
  197.4 43.9 reduce-scatter.11
  244.5 43.9 reduce-scatter.9
  291.5 49.9 reduce-scatter.7
